TPU v7x, 256 devices: a whole 4x4x8 slice. The times are simulated.
256 devices in a mesh: row: 8 (over y_lo, x), col: 32 (over z, y_hi, core).
Axes of the slice: x: 4, y: 4 (y_hi: 2, y_lo: 2; y = y_hi * 2 + y_lo), z: 8, core: 2. Of those that a mesh axis runs over, the one named last changes fastest.
Arguments:
- amplitudes: bfloat16 [800, 640000], P('col', 'row'), may hold values from -6 to 6
- singles: bfloat16 [100, 800], P(None, 'col'), may hold values from -3 to 3
- integrals: bfloat16 [800, 1280000], P('col', 'row'), may hold values from -0.01953125 to 0.01953125
- virt_irrep: int32 [32], replicated, may hold values from 0 to 7
- occ_irrep: int32 [100], replicated, may hold values from 0 to 7
Outputs:
- ladder: bfloat16 [800, 2, 800], P('row', None, 'col')
Inputs may be any that keep to these rules, and one draw needn't show every extreme that they name: `virt_irrep`: irreps of the point group. `occ_irrep`: irreps of the point group.
All inputs are finite; a program needn't handle non-finite values.
Results may differ from a plain program's by a relative error of at most 0.0049.
Values may be sent and summed in bfloat16 or wider, within the bound.
A program may use at most 128 MiB of HBM per device.

v0:
```python
import jax
import jax.numpy as jnp
from jax import lax
from jax.sharding import PartitionSpec as P

VB = 25


def body(amplitudes, singles, integrals, virt_irrep, occ_irrep):
    row_count = lax.axis_size("row")
    col_count = lax.axis_size("col")
    row_index = lax.axis_index("row")
    col_index = lax.axis_index("col")
    second_width = amplitudes.shape[0]
    virt_total = second_width * col_count
    first_width = virt_total // row_count
    pair_count = amplitudes.shape[1] // first_width
    panel_width = integrals.shape[1] // (first_width * virt_total)
    occ_count = occ_irrep.shape[0]
    window_occ = pair_count // occ_count
    orbital_irrep = jnp.repeat(virt_irrep, VB, total_repeat_length=virt_total)
    first_irrep = lax.dynamic_slice_in_dim(orbital_irrep, row_index * first_width, first_width)
    second_irrep = lax.dynamic_slice_in_dim(orbital_irrep, col_index * second_width, second_width)
    panel_irrep = orbital_irrep[:panel_width]
    outer_irrep = jnp.bitwise_xor(panel_irrep[:, None], orbital_irrep[None, :]).reshape(
        panel_width * virt_total
    )
    pair_irrep = jnp.bitwise_xor(occ_irrep[:window_occ][:, None], occ_irrep[None, :]).reshape(
        pair_count
    )
    whole_singles = lax.all_gather(singles, "col", axis=1, tiled=True)
    first_single = lax.dynamic_slice_in_dim(
        whole_singles[:window_occ], row_index * first_width, first_width, 1
    ).astype(jnp.float32)
    second_single = jnp.transpose(singles.astype(jnp.float32))
    outer_part = (
        second_single[:, None, None, :] * jnp.transpose(first_single)[None, :, :, None]
    ).reshape(second_width, first_width, pair_count)
    allowed = (
        jnp.bitwise_xor(
            jnp.bitwise_xor(second_irrep[:, None, None], first_irrep[None, :, None]),
            pair_irrep[None, None, :],
        )
        == 0
    )
    amp_three = amplitudes.reshape(second_width, first_width, pair_count)
    combined = jnp.where(allowed, amp_three.astype(jnp.float32) + outer_part, 0.0).astype(
        jnp.bfloat16
    )
    int_three = integrals.reshape(second_width, first_width, panel_width * virt_total)
    int_allowed = (
        jnp.bitwise_xor(
            jnp.bitwise_xor(second_irrep[:, None, None], first_irrep[None, :, None]),
            outer_irrep[None, None, :],
        )
        == 0
    )
    blocked = jnp.where(int_allowed, int_three, jnp.zeros((), jnp.bfloat16))
    partial_value = lax.dot_general(
        combined.reshape(second_width * first_width, pair_count),
        blocked.reshape(second_width * first_width, panel_width * virt_total),
        (((0,), (0,)), ((), ())),
        preferred_element_type=jnp.float32,
    )
    partial_value = partial_value.reshape(pair_count, panel_width, virt_total)
    reduced = lax.psum_scatter(partial_value, "col", scatter_dimension=2, tiled=True)
    result = lax.psum_scatter(reduced, "row", scatter_dimension=0, tiled=True)
    return result.astype(jnp.bfloat16)


def solution(mesh):
    placed = (P("col", "row"), P(None, "col"), P("col", "row"), P(), P())
    return jax.shard_map(
        body, mesh=mesh, in_specs=placed, out_specs=P("row", None, "col"), check_vma=False
    )
```

profile of v0, /device:TPU:1, one launch (start us, length us, event | category | flops | bytes accessed | tf_op | source)
XLA Modules:
  0.0 503.4 jit_solution(12271829877604401669)
XLA Ops:
  6.5 0.0 all-reduce.5.cloned.1.call-start
  6.5 2.1 fusion.4
  8.6 1.8 fusion.5
  10.4 21.0 %select_select_fusion = s32[800]{0:T(1024)S(1)} fusion(pred[800]{0:T(1024)(128)(4,1)} %constant.143, pred[800]{0:T(1024)(128)(4,1)} %constant.144, pred[800]{0:T(1024)(128)(4,1)} %constant.145, pred[800]{0:T(1024)(128)(4,1)} %constant.146, pred[800]{0:T(1024)(128)(4,1)} %constant.147, pred[800]{0:T(1024)(128)(4,1)} %constant.148, ...), kind=kLoop, calls=%fused_computation.12 | loop fusion | flops 24800 | bytes 28128 | tf_op jit(solution)/shard_map/jit(_take)/gather | solution.py:21
  31.5 0.0 copy-start.1
  31.5 0.1 dynamic_slice.10
  31.6 0.1 dynamic_slice.9
  31.6 0.1 broadcast_xor_fusion
  31.7 4.3 xor.112
  36.0 9.7 %xor.113 = s32[25,80000]{1,0:T(8,128)} reshape(s32[25,100,800]{2,1,0:T(8,128)} %xor.112) | data formatting | bytes 16000000 | tf_op jit(solution)/shard_map/xor | solution.py:40
  45.7 0.0 copy-done.1
  45.7 0.0 copy-done
  45.7 46.9 %all-gather = bf16[32,25,100]{2,1,0:T(8,128)(2,1)S(1)} all-gather(bf16[1,25,100]{2,1,0:T(8,128)(2,1)S(1)} %bitcast.55), channel_id=1, replica_groups=mesh['row'=8,'col'=32] {'col'}, dimensions={0}, use_global_device_ids=true | all-gather | bytes 165000 | tf_op jit(solution)/shard_map/all_gather | solution.py:31
  92.6 0.1 reshape.186
  92.7 0.2 mul.39
  92.9 0.5 mul.40
  93.4 0.1 mul.36
  93.5 4.1 mul.37
  97.6 9.6 %mul.38 = f32[25,80000]{1,0:T(8,128)} reshape(f32[25,100,800]{2,1,0:T(8,128)} %mul.37) | data formatting | bytes 16000000 | tf_op jit(solution)/shard_map/mul | solution.py:37
  107.2 0.0 copy-done.3
  107.2 0.1 broadcast_xor_fusion.2
  107.2 0.1 xor.117
  107.4 0.3 xor.119
  107.6 11.7 %select_convert_fusion = bf16[25,80000]{1,0:T(8,128)(2,1)} fusion(f32[25,80000]{1,0:T(8,128)} %mul.38, bf16[25,80000]{1,0:T(8,128)(2,1)} %param.7, s32[25,80000]{1,0:T(8,128)} %xor.113, f32[80000]{0:T(1024)S(1)} %mul.40, s32[80000]{0:T(1024)S(1)} %xor.119), kind=kLoop, calls=%fused_computation.2 | loop fusion | flops 14000000 | bytes 24640000 | tf_op jit(solution)/shard_map/convert_element_type | solution.py:47
  119.4 8.0 %convert_element_type.19 = bf16[2500,800]{1,0:T(8,128)(2,1)} reshape(bf16[25,80000]{1,0:T(8,128)(2,1)} %select_convert_fusion) | data formatting | bytes 8000000 | tf_op jit(solution)/shard_map/convert_element_type | solution.py:47
  127.4 0.1 xor.124
  127.5 0.1 xor.109
  127.6 0.1 xor.122
  127.7 0.0 copy-done.2
  127.7 0.0 slice-done
  127.7 0.1 broadcast_xor_fusion.1
  127.8 0.1 xor.130
  127.9 15.4 %reshape.145 = bf16[2500,1600]{1,0:T(8,128)(2,1)} reshape(bf16[25,160000]{1,0:T(8,128)(2,1)} %param.9) | data formatting | bytes 16000000 | tf_op jit(solution)/shard_map/reshape | solution.py:50
  143.2 8.3 %fusion.1 = bf16[1600,2500]{0,1:T(8,128)(2,1)} fusion(bf16[2500,1600]{1,0:T(8,128)(2,1)} %reshape.145, s32[1600]{0:T(1024)S(1)} %xor.130, s32[2500]{0:T(1024)S(1)} %xor.125), kind=kLoop, calls=%fused_computation.4 | loop fusion | flops 12000000 | bytes 16016400 | tf_op jit(solution)/shard_map/dot_general | solution.py:59
  151.5 12.1 %copy.20 = bf16[1600,2500]{1,0:T(8,128)(2,1)} copy(bf16[1600,2500]{0,1:T(8,128)(2,1)} %fusion.1) | data formatting | bytes 16000000 | tf_op jit(solution)/shard_map/dot_general | solution.py:59
  163.7 12.7 %fusion.2 = f32[800,2,800]{0,2,1:T(8,128)S(1)} fusion(bf16[2,800,2500]{2,1,0:T(8,128)(2,1)} %bitcast.53, bf16[2500,800]{1,0:T(8,128)(2,1)} %convert_element_type.19), kind=kOutput, calls=%fused_computation.5 | convolution fusion | flops 6400000000 | bytes 17120000 | tf_op jit(solution)/shard_map/dot_general | solution.py:59
  176.4 0.0 copy-start.5
  176.4 0.0 copy-start.4
  176.4 7.0 %copy.22 = f32[800,2,800]{0,1,2:T(2,128)} copy(f32[800,2,800]{0,2,1:T(8,128)S(1)} %fusion.2) | data formatting | bytes 10240000 | tf_op jit(solution)/shard_map/dot_general | solution.py:59
  183.4 0.0 all-reduce.5.cloned.1.call-update
  183.4 0.0 copy-done.5
  183.4 0.6 dynamic-slice.6
  184.0 0.6 dynamic-slice.8
  186.0 280.6 %all-reduce.5.cloned.1.call-done = f32[800,2,800]{0,1,2:T(2,128)} async-done(((f32[800,2,800]{0,1,2:T(2,128)}), f32[800,2,800]{0,1,2:T(2,128)}) %all-reduce.5.cloned.1.call-update) | async-done | bytes 5120016
  466.6 0.9 constant_dynamic-slice_fusion
  467.6 28.3 %all-reduce.6 = bf16[800,2,25]{0,2,1:T(8,128)(2,1)S(1)} all-reduce(f32[800,2,25]{0,2,1:T(8,128)S(1)} %copy.23), channel_id=3, replica_groups=mesh['row'=8,'col'=32] {'row'}, use_global_device_ids=true, to_apply=%region_1.2.clone | all-reduce | flops 40000 | bytes 240000
  495.8 0.1 dynamic-slice_convert_fusion
  495.9 0.6 copy.24
  (12 shorter events, 0.1 us)
Async XLA Ops:
  6.5 460.1 %all-reduce.5.cloned.1.call-start = ((), (), s32[]{:S(2)}) async-start(), calls=%async_computation | async-start | bytes 11468800
  31.5 14.2 %copy-start.1 = (s32[800]{0:T(1024)}, s32[800]{0:T(1024)S(1)}, u32[]{:S(2)}) copy-start(s32[800]{0:T(1024)S(1)} %select_select_fusion) | copy-start | bytes 9604
  36.0 9.7 %copy-start = (bf16[100,25]{0,1:T(8,128)(2,1)S(1)}, bf16[100,25]{0,1:T(8,128)(2,1)}, u32[]{:S(2)}) copy-start(bf16[100,25]{0,1:T(8,128)(2,1)} %param.8) | copy-start | bytes 15004
  97.6 9.6 %copy-start.3 = (s32[100]{0:T(128)S(1)}, s32[100]{0:T(128)}, u32[]{:S(2)}) copy-start(s32[100]{0:T(128)} %param.11) | copy-start | bytes 1204
  119.4 8.3 %copy-start.2 = (s32[800]{0:T(1024)S(1)}, s32[800]{0:T(1024)}, u32[]{:S(2)}) copy-start(s32[800]{0:T(1024)} %copy-done.1) | copy-start | bytes 9604
  119.4 8.3 %slice-start = ((s32[800]{0:T(1024)}), s32[2]{0:T(128)S(1)}, s32[]{:S(2)}) async-start(s32[800]{0:T(1024)} %copy-done.1), calls=%async_computation.1 | async-start | bytes 1024 | tf_op jit(solution)/shard_map/slice | solution.py:24
  176.4 7.0 %copy-start.5 = (u32[256]{0:T(256)S(1)}, u32[256]{0:T(256)}, u32[]{:S(2)}) copy-start(u32[256]{0:T(256)} %constant.178) | copy-start | bytes 3076
  176.4 7.6 %copy-start.4 = (u32[256]{0:T(256)S(1)}, u32[256]{0:T(256)}, u32[]{:S(2)}) copy-start(u32[256]{0:T(256)} %constant.182) | copy-start | bytes 3076
Sparse Core Ops, SparseCore 0:
  183.5 283.0 all-reduce.4
where the time goes:
time: 510 us; the launch traced here: 503 us
  waiting for transfers between devices  281 us (55%)
  local copies, waits for them, and re-layouts  78.7 us (15%)
  blocking collectives  75.2 us (15%)
  other arithmetic  41.3 us (8%)
  between operations  14.9 us (3%)
  matrix products  12.7 us (2%)
    unnamed x2, waiting for transfers between devices  281 us
    all_gather x1, blocking collectives, body(): whole_singles = lax.all_gather(singles, 'col', axis=1, tiled=True)  46.9 us
    unnamed x1, blocking collectives  28.3 us
    gather x1, other arithmetic, body(): orbital_irrep = jnp.repeat(virt_irrep, VB, total_repeat_length=virt_total)  21 us
    dot_general x2, local copies, waits for them, and re-layouts, body(): lax.dot_general(combined.reshape(second_width * first_width, pair_count),...  19.1 us
    reshape x1, local copies, waits for them, and re-layouts, body(): integrals.reshape(second_width, first_width, panel_width * virt_total)  15.4 us
    mul x6, local copies, waits for them, and re-layouts, body(): second_single[:, None, None, :]  14.4 us
    xor x4, local copies, waits for them, and re-layouts, body(): jnp.bitwise_xor(jnp.bitwise_xor(second_irrep[:, None, None], first_irrep[...  14.2 us
  transfers between devices with their start and end apart: 1, of which 1 were waited for; matrix products, arithmetic and copies ran while one was open for 0% of the time, Pallas kernels for 0%

commit v1 on v0

v1 whole, which is shorter than its diff:
```python
import functools

import jax
import jax.numpy as jnp
from jax import lax
from jax.experimental import pallas as pl
from jax.experimental.pallas import tpu as pltpu
from jax.sharding import PartitionSpec as P

MESH = pl.DeviceIdType.MESH
BF = jnp.bfloat16
F32 = jnp.float32
I32 = jnp.int32

VB = 25
NB = 32
NOCC = 100
PI = 8
NV = 800
ROWS, COLS = 8, 32
NC = 100
SLOT = 32
WIN = 896
ALEN = 157 * 128
KP = 1792
TILES = ((0, 256), (256, 256), (512, 256), (768, 128))


def iota(shape, dim):
    return lax.broadcasted_iota(I32, shape, dim)


def pad_rows(x):
    return jnp.concatenate([x, jnp.zeros((32 - x.shape[0], x.shape[1]), x.dtype)], axis=0)


def kernel(
    round_ref, virt, occ, occ_row, singles, amp, integ,
    out, rounds_out,
    av, bv, enc, onehot, cs, ct, masks, acc, sj, sc, s_own, s_in, expand,
    core_out, core_in, qf, qb, row_in, wsum, zb, zf, col_in, res,
    asem, bsem, ssend, srecv, csend, crecv, rsend, rrecv, zsend, zrecv,
):
    r = lax.axis_index("row")
    c = lax.axis_index("col")
    core = lax.rem(c, 2)
    partner = c + 1 - 2 * core

    def amp_copy(q):
        return pltpu.make_async_copy(
            amp.at[:, pl.ds(q * (156 * 128), ALEN)], av.at[q], asem.at[q]
        )

    for q in range(4):
        amp_copy(q).start()

    def int_copy(a, k):
        src = pl.multiple_of(128 * ((25 * k - lax.rem(k, 2)) // 2 + 6 * a), 128)
        dst = pl.multiple_of(k * WIN, 128)
        return pltpu.make_async_copy(
            integ.at[:, pl.ds(src, WIN)], bv.at[a, :, pl.ds(dst, WIN)], bsem.at[a]
        )

    for a in range(2):
        def start_int(k, carry, a=a):
            int_copy(a, k).start()
            return carry
        lax.fori_loop(0, NC, start_int, 0)

    barrier = pltpu.get_barrier_semaphore()
    mate_row = c // 4
    far = r != mate_row

    def greet_col(k, carry):
        pl.semaphore_signal(
            barrier, inc=1, device_id=(r, lax.rem(c + k, COLS)), device_id_type=MESH
        )
        return carry

    lax.fori_loop(1, COLS, greet_col, 0)

    def greet_row(k, carry):
        pl.semaphore_signal(
            barrier, inc=1, device_id=(lax.rem(r + k, ROWS), c), device_id_type=MESH
        )
        return carry

    lax.fori_loop(1, ROWS, greet_row, 0)

    @pl.when(far)
    def _():
        for q in range(4):
            pl.semaphore_signal(
                barrier, inc=1, device_id=(mate_row, 4 * r + q), device_id_type=MESH
            )

    first_rank = round_ref[0] * SLOT
    lane = iota((128, 128), 1)
    sub = iota((128, 128), 0)
    h_row = jnp.concatenate([occ_row[...], jnp.full((1, 128 - NOCC), 99, I32)], axis=1)
    h_lane = jnp.broadcast_to(h_row, (128, 128))
    h_sub = h_lane.T
    same = h_lane == h_sub
    rank_sub = jnp.sum(
        jnp.where(same & (lane < sub), 1.0, 0.0), axis=1, keepdims=True
    ).astype(I32)
    rank_lane = jnp.sum(
        jnp.where(same & (sub < lane), 1.0, 0.0), axis=0, keepdims=True
    ).astype(I32)
    top = jnp.max(jnp.where(sub < NOCC, jnp.broadcast_to(rank_sub, (128, 128)), 0))
    rounds_out[0] = (top >> 5) + 1
    rk = jnp.broadcast_to(rank_sub, (128, 128)) - first_rank
    fits = (rk >= 0) & (rk < SLOT) & (sub < NOCC)
    code = jnp.where(fits, ((rk >> 4) << 7) + (rk & 15), -4096)
    enc[pl.ds(0, 96), :] = jnp.full((96, 128), -1, I32)
    enc[pl.ds(896, 96), :] = jnp.full((96, 128), -1, I32)
    il = (lane >> 4)
    hl = jnp.zeros((128, 128), I32)
    for i in range(PI):
        hi = occ[i]
        hl = jnp.where(il == i, hi, hl)
        value = jnp.where(fits, ((h_sub ^ hi) << 10) + code + 16 * i, -1)
        enc[pl.ds(96 + 100 * i, 100), :] = value[0:100, :]

    g_own = virt[c]
    g_zero = virt[0]

    def class_of(q):
        return virt[4 * r + q] ^ g_own

    s_pad = pad_rows(
        jnp.concatenate([singles[...], jnp.zeros((VB, 128 - NOCC), BF)], axis=1)
    )
    s_own[...] = s_pad

    for q in range(4):
        kq = class_of(q)
        pair_ok = (h_sub ^ hl) == kq
        parts = [
            jnp.where(pair_ok & (code + (il << 4) == lane + 128 * half), 1.0, 0.0).astype(BF)
            for half in range(2)
        ]
        sj[q] = jnp.dot(
            s_pad, jnp.concatenate(parts, axis=1), preferred_element_type=F32
        )

    esub = iota((SLOT, 128), 0)
    elane = iota((SLOT, 128), 1)
    keep = (
        ((h_lane[0:SLOT, :] ^ occ[r]) == (g_zero ^ g_own))
        & (jnp.broadcast_to(rank_lane, (SLOT, 128)) - first_rank == esub)
        & (elane < NOCC)
    )
    expand[...] = jnp.where(keep, 1.0, 0.0).astype(BF)

    def build(step, carry):
        q = step // 2
        start = pl.multiple_of(lax.rem(step, 2) * 496, 16)
        kq = virt[4 * r + q] ^ g_own
        e = enc[pl.ds(start, 496), :]
        l2 = iota((496, 128), 1) + (kq << 10)
        o0 = jnp.where(e == l2, 1.0, 0.0).astype(BF)
        o1 = jnp.where(e == l2 + 128, 1.0, 0.0).astype(BF)
        onehot[q, pl.ds(start, 496), 0:128] = o0
        onehot[q, pl.ds(start, 496), 128:256] = o1
        return carry

    lax.fori_loop(0, 8, build, 0)

    vrow = iota((8, WIN), 0)
    shift = ((vrow & 1) << 6) + (((vrow >> 1) & 1) << 5)
    b_lane = iota((8, WIN), 1) - shift
    inside = (b_lane >= 0) & (b_lane < NV)
    blk = (jnp.where(inside, b_lane, 0) * 5243) >> 17
    g_lane = jnp.full((8, WIN), 99, I32)
    for k in range(NB):
        g_lane = jnp.where(blk == k, virt[k], g_lane)
    g_lane = jnp.where(inside, g_lane, 99)
    for v in range(4):
        for q in range(4):
            want = g_zero ^ class_of(q)
            row = jnp.broadcast_to(g_lane[v : v + 1, :], (32, WIN))
            masks[v, q] = jnp.where(row == want, 1.0, 0.0).astype(BF)

    pl.semaphore_wait(barrier, COLS - 1 + ROWS - 1 + 4 * far.astype(I32))
    my_q = lax.rem(c, 4)

    def singles_copy(t):
        return pltpu.make_async_remote_copy(
            src_ref=s_own,
            dst_ref=s_in.at[my_q],
            send_sem=ssend.at[t],
            recv_sem=srecv.at[my_q],
            device_id=(mate_row, 4 * r + t),
            device_id_type=MESH,
        )

    def singles_wait(t):
        return pltpu.make_async_remote_copy(
            src_ref=s_own,
            dst_ref=s_in.at[t],
            send_sem=ssend.at[t],
            recv_sem=srecv.at[t],
            device_id=(mate_row, 4 * r + t),
            device_id_type=MESH,
        )

    for t in range(4):
        other = far | (my_q != t)

        @pl.when(other)
        def _():
            singles_copy(t).start()

        @pl.when(jnp.logical_not(other))
        def _():
            s_in[t] = s_own[...]

    fsub = iota((128, 256), 0)
    pick = jnp.where(fsub == ((iota((128, 256), 1) & 127) >> 4), 1.0, 0.0).astype(BF)
    for t in range(4):
        other = far | (my_q != t)

        @pl.when(other)
        def _():
            singles_wait(t).wait_send()
            singles_wait(t).wait_recv()

        sc[t] = jnp.dot(s_in[t], pick, preferred_element_type=F32)

    for p in range(2):
        cs[p, 1600:KP, :] = jnp.zeros((KP - 1600, 256), BF)

    def compact(q, carry):
        amp_copy(q).wait()
        for u0 in range(4):
            count = 7 if u0 == 0 else 6
            res4 = lax.rem(q + u0, 4)
            step = (q + u0) // 4
            pieces = []
            for w in range(count):
                base = pl.multiple_of(128 * (25 * w + 6 * u0 + step), 128)
                pieces.append(pad_rows(av[q, :, pl.ds(base, WIN)]))
            left = jnp.concatenate(pieces, axis=0)
            start = pl.multiple_of(96 - 32 * res4, 32)
            got = jnp.dot(
                left, onehot[q, pl.ds(start, WIN), :], preferred_element_type=F32
            )
            par = lax.rem(q + u0, 2)
            half = (25 * q + u0) // 2
            for w in range(count):
                u = u0 + 4 * w
                value = got[32 * w : 32 * w + 32, :] + sc[q, u : u + 1, :] * sj[q]
                at = pl.multiple_of(32 * (half + 2 * w), 32)
                cs[par, pl.ds(at, 32), :] = value.astype(BF)
        return carry

    lax.fori_loop(0, 4, compact, 0)

    def turn(step, carry):
        p = step // 7
        at = pl.multiple_of(lax.rem(step, 7) * 256, 256)
        ct[p, :, pl.ds(at, 256)] = cs[p, pl.ds(at, 256), :].T
        return carry

    lax.fori_loop(0, 14, turn, 0)

    def main_tile(a, lane0, width):
        for p in range(2):
            m = [masks[2 * a + p, q, 0:VB, pl.ds(lane0, width)] > 0 for q in range(4)]
            pieces = []
            for w in range(50):
                k = 2 * w + p
                x = bv[a, :, pl.ds(k * WIN + lane0, width)]
                pieces.append(pad_rows(jnp.where(m[k // 25], x, jnp.zeros_like(x))))
            pieces.append(jnp.zeros((KP - 1600, width), BF))
            right = jnp.concatenate(pieces, axis=0)
            acc[a, p, :, pl.ds(lane0, width)] = jnp.dot(
                ct[p], right, preferred_element_type=F32
            )

    def main_range(a, lo, hi):
        def one(n, carry):
            main_tile(a, pl.multiple_of(n * 256, 256), 256)
            return carry
        lax.fori_loop(lo, hi, one, 0)

    def core_copy(a):
        return pltpu.make_async_remote_copy(
            src_ref=core_out.at[a], dst_ref=core_in.at[a],
            send_sem=csend.at[a], recv_sem=crecv.at[a],
            device_id=(r, partner), device_id_type=MESH,
        )

    def row_copy(a, k):
        to = lax.rem(r + k, ROWS)
        return pltpu.make_async_remote_copy(
            src_ref=qb.at[a, pl.ds(pl.multiple_of(16 * to, 16), 16), :],
            dst_ref=row_in.at[a, k - 1],
            send_sem=rsend.at[a, k - 1], recv_sem=rrecv.at[a, k - 1],
            device_id=(to, c), device_id_type=MESH,
        )

    def wait_int(a):
        pltpu.make_async_copy(bv.at[a], bv.at[a], bsem.at[a]).wait()

    def join(a):
        odd = acc[a, 1]
        odd = jnp.concatenate([odd[:, 64:], jnp.zeros((256, 64), F32)], axis=1)
        acc[a, 0] = acc[a, 0] + odd
        give = pl.multiple_of((1 - core) * 128, 128)
        core_out[a] = acc[a, 0, pl.ds(give, 128), :].astype(BF)
        core_copy(a).start()

    def spread(a):
        core_copy(a).wait()
        keep_at = pl.multiple_of(core * 128, 128)
        total = acc[a, 0, pl.ds(keep_at, 128), :] + core_in[a].astype(F32)
        qf[a] = total
        qb[a] = total.astype(BF)
        for k in range(1, ROWS):
            row_copy(a, k).start()

    wait_int(0)
    main_range(0, 0, 3)
    main_tile(0, 768, 128)
    join(0)
    wait_int(1)
    main_range(1, 0, 2)
    spread(0)
    main_range(1, 2, 3)
    main_tile(1, 768, 128)
    join(1)
    spread(1)

    for a in range(2):
        total = qf[a, pl.ds(pl.multiple_of(16 * r, 16), 16), :]
        for k in range(1, ROWS):
            row_copy(a, k).wait()
            total = total + row_in[a, k - 1].astype(F32)
        wsum[a] = total

    zlane = iota((16, 128), 1)
    for t in range(16):
        sides = []
        for a in range(2):
            begin = 32 * a + 50 * t
            tile, s = begin // 128, begin % 128
            to = 64 * a
            turn_by = (to - s) % 128
            x = wsum[a, :, tile * 128 : tile * 128 + 128]
            if turn_by:
                x = pltpu.roll(x, turn_by, 1)
            if s + 50 > 128:
                y = wsum[a, :, tile * 128 + 128 : tile * 128 + 256]
                if turn_by:
                    y = pltpu.roll(y, turn_by, 1)
                x = jnp.where(zlane - to + s < 128, x, y)
            sides.append(x)
        z = jnp.where(zlane < 64, sides[0], sides[1])
        zf[t] = z
        zb[t] = z.astype(BF)

    def col_copy(k):
        to = lax.rem(c + k, COLS)
        return pltpu.make_async_remote_copy(
            src_ref=zb.at[to // 2], dst_ref=col_in.at[k - 1],
            send_sem=zsend.at[k - 1], recv_sem=zrecv.at[k - 1],
            device_id=(r, to), device_id_type=MESH,
        )

    def start_col(k, carry):
        col_copy(k).start()
        return carry

    lax.fori_loop(1, COLS, start_col, 0)
    mine = zf[c // 2]
    other = jnp.zeros((16, 128), F32)
    for k in range(1, COLS):
        col_copy(k).wait()
        part = col_in[k - 1].astype(F32)
        if k % 2:
            other = other + part
        else:
            mine = mine + part
    res[pl.ds(pl.multiple_of(core * 16, 16), 16), :] = mine
    res[pl.ds(pl.multiple_of((1 - core) * 16, 16), 16), :] = other

    osub = iota((64, 128), 0)
    b_own = osub & 31
    wanted = ((osub >> 5) << 6) + core * VB + b_own
    select = jnp.where((iota((64, 128), 1) == wanted) & (b_own < VB), 1.0, 0.0).astype(BF)
    narrow = lax.dot_general(
        select, res[...].astype(BF), (((1,), (1,)), ((), ())), preferred_element_type=F32
    ).astype(BF)
    final = jnp.dot(narrow, expand[...], preferred_element_type=F32).astype(BF)
    for a in range(2):
        out[a] = final[32 * a : 32 * a + VB, 0:NOCC]


def run_round(index, amplitudes, singles_t, integrals, virt_irrep, occ_irrep):
    smem = pl.BlockSpec(memory_space=pltpu.SMEM)
    vmem = pl.BlockSpec(memory_space=pltpu.VMEM)
    hbm = pl.BlockSpec(memory_space=pl.ANY)
    dma = pltpu.SemaphoreType.DMA
    return pl.pallas_call(
        kernel,
        out_shape=(
            jax.ShapeDtypeStruct((2, VB, NOCC), BF),
            jax.ShapeDtypeStruct((1,), I32),
        ),
        in_specs=[smem, smem, smem, vmem, vmem, hbm, hbm],
        out_specs=(vmem, smem),
        scratch_shapes=[
            pltpu.VMEM((4, VB, ALEN), BF),
            pltpu.VMEM((2, VB, NC * WIN), BF),
            pltpu.VMEM((992, 128), I32),
            pltpu.VMEM((4, 992, 256), BF),
            pltpu.VMEM((2, KP, 256), BF),
            pltpu.VMEM((2, 256, KP), BF),
            pltpu.VMEM((4, 4, 32, WIN), BF),
            pltpu.VMEM((2, 2, 256, WIN), F32),
            pltpu.VMEM((4, 32, 256), F32),
            pltpu.VMEM((4, 32, 256), F32),
            pltpu.VMEM((32, 128), BF),
            pltpu.VMEM((4, 32, 128), BF),
            pltpu.VMEM((SLOT, 128), BF),
            pltpu.VMEM((2, 128, WIN), BF),
            pltpu.VMEM((2, 128, WIN), BF),
            pltpu.VMEM((2, 128, WIN), F32),
            pltpu.VMEM((2, 128, WIN), BF),
            pltpu.VMEM((2, ROWS - 1, 16, WIN), BF),
            pltpu.VMEM((2, 16, WIN), F32),
            pltpu.VMEM((16, 16, 128), BF),
            pltpu.VMEM((16, 16, 128), F32),
            pltpu.VMEM((COLS - 1, 16, 128), BF),
            pltpu.VMEM((SLOT, 128), F32),
            dma((4,)), dma((2,)), dma((4,)), dma((4,)), dma((2,)), dma((2,)),
            dma((2, ROWS - 1)), dma((2, ROWS - 1)), dma((COLS - 1,)), dma((COLS - 1,)),
        ],
        compiler_params=pltpu.CompilerParams(
            collective_id=0, has_side_effects=True, vmem_limit_bytes=50 * 1024 * 1024
        ),
        name="ladder_round",
    )(
        index, virt_irrep, occ_irrep, occ_irrep.reshape(1, NOCC), singles_t,
        amplitudes, integrals,
    )


def body(amplitudes, singles, integrals, virt_irrep, occ_irrep):
    singles_t = jnp.transpose(singles)

    def more(state):
        return state[0] < state[1][0]

    def step(state):
        index, _, total = state
        part, rounds = run_round(
            jnp.full((1,), index, I32), amplitudes, singles_t, integrals, virt_irrep, occ_irrep
        )
        return index + 1, rounds, total + part

    start = (jnp.int32(0), jnp.ones((1,), I32), jnp.zeros((2, VB, NOCC), BF))
    _, _, total = lax.while_loop(more, step, start)
    return jnp.transpose(total, (2, 0, 1))


def solution(mesh):
    placed = (P("col", "row"), P(None, "col"), P("col", "row"), P(), P())
    return jax.shard_map(
        body, mesh=mesh, in_specs=placed, out_specs=P("row", None, "col"), check_vma=False
    )
```

time: 510 us -> 49 us (0.10); the launches traced: 503 us -> 48.9 us
  waiting for transfers between devices: 281 us -> 0 us
  local copies, waits for them, and re-layouts: 78.7 us -> 0.62 us
  blocking collectives: 75.2 us -> 0 us
  Pallas kernels: 0 us -> 47.6 us
  other arithmetic: 41.3 us -> 0.02 us
  between operations: 14.9 us -> 0.01 us
  matrix products: 12.7 us -> 0 us
    unnamed x2 -> x0, waiting for transfers between devices: 281 us -> none
    pallas_call x0 -> x1, Pallas kernels: none -> 47.6 us  [run_round(): pl.pallas_call(kernel, out_shape=(jax.ShapeDtypeStruct((2, VB, NOCC), BF)...]
    all_gather x1 -> x0, blocking collectives: 46.9 us -> none  [body(): whole_singles = lax.all_gather(singles, 'col', axis=1, tiled=True)]
    unnamed x1 -> x0, blocking collectives: 28.3 us -> none
    gather x1 -> x0, other arithmetic: 21 us -> none  [body(): orbital_irrep = jnp.repeat(virt_irrep, VB, total_repeat_length=virt_total)]
    dot_general x2 -> x0, local copies, waits for them, and re-layouts: 19.1 us -> none  [body(): lax.dot_general(combined.reshape(second_width * first_width, pair_count),...]
    reshape x1 -> x0, local copies, waits for them, and re-layouts: 15.4 us -> none  [body(): integrals.reshape(second_width, first_width, panel_width * virt_total)]
    xor x10 -> x0, local copies, waits for them, and re-layouts: 14.7 us -> none  [the longest x4 14.2 us: body(): jnp.bitwise_xor(jnp.bitwise_xor(second_irrep[:, None, None], first_irrep[...]
  transfers between devices with their start and end apart: 1 -> 0, of which waited for: 1 -> 0; matrix products, arithmetic and copies ran while one was open for 0% -> 0% of each run, Pallas kernels for 0% -> 0%
where the time goes in v1:
time: 49 us; the launch traced here: 48.9 us
  Pallas kernels  47.6 us (97%)
  loops' own time  0.65 us (1%)
  local copies, waits for them, and re-layouts  0.62 us (1%)
    pallas_call x1, Pallas kernels, run_round(): pl.pallas_call(kernel, out_shape=(jax.ShapeDtypeStruct((2, VB, NOCC), BF)...  47.6 us

profile of v1, /device:TPU:1, one launch (start us, length us, event | category | flops | bytes accessed | tf_op | source)
XLA Modules:
  0.0 48.9 jit_solution(2159785350653531049)
XLA Ops:
  0.0 48.2 %while.12 = (s32[]{:T(128)}, s32[1]{0:T(128)}, bf16[2,25,100]{2,1,0:T(8,128)(2,1)S(1)}, s32[100]{0:T(128)}, s32[32]{0:T(128)}, /*index=5*/bf16[25,100]{1,0:T(8,1...) while((s32[]{:T(128)}, s32[1]{0:T(128)}, bf16[2,25,100]{2,1,0:T(8,128)(2,1)S(1)}, ...), condition=%wide.region_1.0_spmd, body=%wide.region_0.0_spmd.sunk | while | flops 5002 | bytes 30101 | solution.py:465
  0.0 47.6 %ladder_round.1 = (bf16[2,25,100]{2,1,0:T(8,128)(2,1)S(1)}, s32[1]{0:T(128)}) custom-call(s32[1]{0:T(128)} %bitcast.10.round_ref, s32[32]{0:T(128)} %get-tuple-element.140.virt, s32[100]{0:T(128)} %get-tuple-element.139.occ, s32[1,100]{1,0:T(1,128)} %bitcast.13, bf16[25,100]{1,0:T(8,128)(2,1)} %get-tuple-element.141.singles, ...), custom_call_target="tpu_custom_call" | custom-call | tf_op jit(solution)/shard_map/while/body/ladder_round/pallas_call | solution.py:406
  48.3 0.6 %copy.8 = bf16[2,25,100]{2,0,1:T(2,128)(2,1)} copy(bf16[2,25,100]{2,1,0:T(8,128)(2,1)S(1)} %get-tuple-element.49) | data formatting | bytes 20000 | tf_op jit(solution)/shard_map/while | solution.py:465
  (2 shorter events, 0.0 us)

commit v2 on v0

v2 whole, which is shorter than its diff:
```python
import functools

import jax
import jax.numpy as jnp
from jax import lax
from jax.experimental import pallas as pl
from jax.experimental.pallas import tpu as pltpu
from jax.sharding import PartitionSpec as P

MESH = pl.DeviceIdType.MESH
BF = jnp.bfloat16
F32 = jnp.float32
I32 = jnp.int32

VB = 25
NB = 32
NOCC = 100
PI = 8
ROWS, COLS = 8, 32
NC = 100
SLOT = 24
PR = PI * SLOT
WIN = 896
ALEN = 157 * 128
KP = 3328
KH = KP // 2
BCH = 5
BLEN = 20 * 1600
NW = 13 * 128
NV = 800


def iota(shape, dim):
    return lax.broadcasted_iota(I32, shape, dim)


def pad_rows(x):
    return jnp.concatenate([x, jnp.zeros((32 - x.shape[0], x.shape[1]), x.dtype)], axis=0)


def one(cond):
    return jnp.where(cond, 1.0, 0.0).astype(BF)


def kernel(
    round_ref, virt, occ, occ_row, singles, amp, integ,
    out, rounds_out,
    av, bv, enc, onehot, cs, rt, ct, masks, bm, sjx, spread_c, acc, psum, s_own, s_in, expand,
    core_out, core_in, qf, qb, xy_in, zf, zb, z_in,
    asem, bsem, ssend, srecv, csend, crecv, rsend, rrecv, zsend, zrecv,
):
    r = lax.axis_index("row")
    c = lax.axis_index("col")
    x = lax.rem(r, 4)
    y_lo = r // 4
    z = c // 4
    y_hi = lax.rem(c // 2, 2)
    core = lax.rem(c, 2)
    y = 2 * y_hi + y_lo

    def device(x, y, z, core):
        return lax.rem(y, 2) * 4 + x, z * 4 + (y // 2) * 2 + core

    def copy_to(where, src, dst, send, recv):
        return pltpu.make_async_remote_copy(
            src_ref=src, dst_ref=dst, send_sem=send, recv_sem=recv,
            device_id=where, device_id_type=MESH,
        )

    def amp_copy(q):
        return pltpu.make_async_copy(
            amp.at[:, pl.ds(pl.multiple_of(q * (156 * 128), 128), ALEN)], av.at[q], asem.at[q]
        )

    def int_copy(k):
        return pltpu.make_async_copy(
            integ.at[:, pl.ds(pl.multiple_of(k * BLEN, 128), BLEN)], bv.at[k], bsem.at[k]
        )

    for q in range(4):
        amp_copy(q).start()
    for k in range(BCH):
        int_copy(k).start()

    barrier = pltpu.get_barrier_semaphore()
    at_home = r == z
    is_source = x == lax.rem(z, 4)
    target_y = jnp.where(y_lo == z // 4, y, 3 - y)

    def greet(where):
        pl.semaphore_signal(barrier, inc=1, device_id=where, device_id_type=MESH)

    for sy in (y, 3 - y):
        for sc in range(2):
            me = at_home & (sc == core) if sy is y else False
            if sy is y:
                @pl.when(jnp.logical_not(me))
                def _():
                    greet(device(x, sy, r, sc))
            else:
                greet(device(x, sy, r, sc))

    def z_peer(k):
        return device(x, y, lax.rem(z + k, 8), core)

    def z_cross(k):
        return device(x, y, lax.rem(z + k, 8), 1 - core)

    def xy_peer(k):
        return device(lax.rem(x + lax.rem(k, 4), 4), lax.rem(y + k // 4, 4), z, core)

    partner = device(x, y, z, 1 - core)

    def greet_z(k, carry):
        greet(z_peer(k))
        greet(z_cross(k))
        return carry

    def greet_xy(k, carry):
        greet(xy_peer(k))
        return carry

    lax.fori_loop(1, 8, greet_z, 0)
    lax.fori_loop(1, 16, greet_xy, 0)
    greet(partner)

    first_rank = round_ref[0] * SLOT
    lane = iota((128, 128), 1)
    sub = iota((128, 128), 0)
    h_row = jnp.concatenate([occ_row[...], jnp.full((1, 128 - NOCC), 99, I32)], axis=1)
    h_lane = jnp.broadcast_to(h_row, (128, 128))
    h_sub = h_lane.T
    same = h_lane == h_sub
    rank_sub = jnp.broadcast_to(
        jnp.sum(jnp.where(same & (lane < sub), 1.0, 0.0), axis=1, keepdims=True).astype(I32),
        (128, 128),
    )
    rank_lane = jnp.sum(
        jnp.where(same & (sub < lane), 1.0, 0.0), axis=0, keepdims=True
    ).astype(I32)
    top = jnp.max(jnp.where(sub < NOCC, rank_sub, 0))
    rounds_out[0] = sum((top >= SLOT * k).astype(I32) for k in range(5))
    rk = rank_sub - first_rank
    fits = (rk >= 0) & (rk < SLOT) & (sub < NOCC)
    enc[pl.ds(0, 96), :] = jnp.full((96, 128), -1, I32)
    enc[pl.ds(896, 96), :] = jnp.full((96, 128), -1, I32)
    for i in range(PI):
        code = jnp.where(rk < 16, rk + 16 * i, rk + (112 + 8 * i))
        value = jnp.where(fits, ((h_sub ^ occ[i]) << 10) + code, -1)
        enc[pl.ds(96 + 100 * i, 100), :] = value[0:100, :]

    g_own = virt[c]
    g_zero = virt[0]

    def build(step, carry):
        q = step // 2
        start = pl.multiple_of(lax.rem(step, 2) * 496, 16)
        kq = virt[4 * r + q] ^ g_own
        e = enc[pl.ds(start, 496), :]
        l2 = iota((496, 128), 1) + (kq << 10)
        onehot[q, pl.ds(start, 496), 0:128] = one(e == l2)
        onehot[q, pl.ds(start, 496), 128:256] = one(e == l2 + 128)
        return carry

    lax.fori_loop(0, 8, build, 0)

    my_q = lax.rem(c, 4)
    s_pad = pad_rows(
        jnp.concatenate([singles[...], jnp.zeros((VB, 128 - NOCC), BF)], axis=1)
    )
    place = one(iota((32, 128), 1) == iota((32, 128), 0) + VB * my_q)
    place = jnp.where(iota((32, 128), 0) < VB, place.astype(F32), 0.0).astype(BF)
    s_own[...] = lax.dot_general(
        s_pad[:, 0:16], place, (((0,), (0,)), ((), ())), preferred_element_type=F32
    ).astype(BF)

    for p in range(2):
        cs[KH * p + 1600 : KH * p + KH, :] = jnp.zeros((KH - 1600, 256), BF)

    def compact(q, carry):
        amp_copy(q).wait()
        for u0 in range(4):
            count = 7 if u0 == 0 else 6
            step = (q + u0) // 4
            pieces = []
            for w in range(count):
                base = pl.multiple_of(128 * (25 * w + 6 * u0 + step), 128)
                pieces.append(pad_rows(av[q, :, pl.ds(base, WIN)]))
            left = jnp.concatenate(pieces, axis=0)
            start = pl.multiple_of(96 - 32 * lax.rem(q + u0, 4), 32)
            got = jnp.dot(
                left, onehot[q, pl.ds(start, WIN), :], preferred_element_type=F32
            ).astype(BF)
            at0 = KH * lax.rem(q + u0, 2) + 32 * ((25 * q + u0) // 2)
            for w in range(count):
                at = pl.multiple_of(at0 + 64 * w, 32)
                cs[pl.ds(at, 32), :] = got[32 * w : 32 * w + 32, :]
        return carry

    lax.fori_loop(0, 4, compact, 0)

    def turn(step, carry):
        at = pl.multiple_of(step * 256, 256)
        rt[:, pl.ds(at, 256)] = cs[pl.ds(at, 256), :].T[0:PR, :]
        return carry

    lax.fori_loop(0, KP // 256, turn, 0)

    pl.semaphore_wait(
        barrier,
        30 + jnp.where(is_source, 16, 0) - jnp.where(is_source & at_home, 1, 0),
    )

    def singles_copy(k):
        tz, tc = k // 2, lax.rem(k, 2)
        return copy_to(
            device(x, target_y, tz, tc), s_own, s_in.at[my_q], ssend.at[k], srecv.at[my_q]
        )

    def not_me(k):
        return jnp.logical_not(at_home & (k // 2 == z) & (lax.rem(k, 2) == core))

    @pl.when(is_source)
    def _():
        def send(k, carry):
            @pl.when(not_me(k))
            def _():
                singles_copy(k).start()
            return carry
        lax.fori_loop(0, 16, send, 0)

    for p in range(2):
        col_at = iota((8, NW), 1) - 64 * p
        b_at = jnp.where(col_at >= NV, col_at - NV, jnp.where(col_at < 0, 0, col_at))
        b_block = (b_at * 5243) >> 17
        g_lane = jnp.full((8, NW), 99, I32)
        for k in range(NB):
            g_lane = jnp.where(b_block == k, virt[k], g_lane)
        g_lane = jnp.where((col_at >= 0) & (col_at < 2 * NV), g_lane, 99)
        for q in range(4):
            want = g_zero ^ g_own ^ virt[4 * r + q]
            masks[p, q] = one(jnp.broadcast_to(g_lane[0:1, :], (32, NW)) == want)

    for p in range(2):
        bm[p, 1600:KH, :] = jnp.zeros((KH - 1600, NW), BF)

    def arrange(k, carry):
        @pl.when(lax.rem(k, 10) == 0)
        def _():
            int_copy(k // 10).wait()
        ch, w = k // 10, lax.rem(k, 10)
        row = pl.multiple_of(32 * k, 32)
        for p in range(2):
            q = (2 * k + p) // 25
            for n in range(13):
                v = bv[ch, :, pl.ds(pl.multiple_of(128 * (25 * w + 12 * p + n), 128), 128)]
                ok = masks[p, q, 0:VB, n * 128 : n * 128 + 128] > 0
                v = jnp.where(ok, v, jnp.zeros_like(v))
                bm[p, pl.ds(row, 32), n * 128 : n * 128 + 128] = pad_rows(v)
        return carry

    lax.fori_loop(0, NC // 2, arrange, 0)

    prow = iota((PR, 128), 0)
    late = prow >= 128
    slot = jnp.where(late, 16 + (prow & 7), prow & 15)
    i_row = jnp.where(late, (prow - 128) >> 3, prow >> 4)
    h_i = jnp.zeros((PR, 128), I32)
    for i in range(PI):
        h_i = jnp.where(i_row == i, occ[i], h_i)
    slot_ok = (jnp.broadcast_to(rank_lane, (PR, 128)) - first_rank) == slot
    pair_class = jnp.broadcast_to(h_row, (PR, 128)) ^ h_i
    s_t = lax.dot_general(
        s_pad, one(iota((32, 128), 0) == (iota((32, 128), 1) & 31)),
        (((0,), (0,)), ((), ())), preferred_element_type=F32,
    ).astype(BF)
    by_class = [
        jnp.dot(
            one(slot_ok & (pair_class == (virt[4 * r + q] ^ g_own))), s_t,
            preferred_element_type=F32,
        )
        for q in range(4)
    ]
    plane = iota((PR, 128), 1)
    for tile in range(KP // 128):
        begin = 8 * (tile % 13) + tile // 13
        low, high = min(3, begin // VB), min(3, (begin + 6) // VB)
        value = by_class[low]
        if low != high:
            value = jnp.where(2 * (plane >> 5) + begin < VB * high, value, by_class[high])
        sjx[:, tile * 128 : tile * 128 + 128] = value
    for p in range(2):
        c_at = 2 * (iota((128, KH), 1) >> 5) + p
        spread_c[:, KH * p : KH * p + KH] = one(iota((128, KH), 0) == c_at)

    erow = iota((32, 128), 0)
    keep = (
        ((h_lane[0:32, :] ^ occ[r]) == (g_zero ^ g_own))
        & (jnp.broadcast_to(rank_lane, (32, 128)) - first_rank == erow)
        & (iota((32, 128), 1) < NOCC)
        & (erow < SLOT)
    )
    expand[...] = one(keep)

    @pl.when(is_source)
    def _():
        def sent(k, carry):
            @pl.when(not_me(k))
            def _():
                singles_copy(k).wait_send()
            return carry
        lax.fori_loop(0, 16, sent, 0)

    for t in range(4):
        me = at_home & (my_q == t)

        @pl.when(jnp.logical_not(me))
        def _():
            copy_to(partner, s_own, s_in.at[t], ssend.at[t], srecv.at[t]).wait_recv()

        @pl.when(me)
        def _():
            s_in[t] = s_own[...]

    pack = s_in[0].astype(F32)
    for t in range(1, 4):
        pack = pack + s_in[t].astype(F32)
    first = jnp.dot(pack.astype(BF), spread_c[...], preferred_element_type=F32)
    for tile in range(KP // 128):
        cols = slice(tile * 128, tile * 128 + 128)
        for block in range(PR // 16):
            rows = slice(16 * block, 16 * block + 16)
            if block < PI:
                left = jnp.broadcast_to(first[block : block + 1, cols], (16, 128))
            else:
                i = 2 * (block - PI)
                left = jnp.concatenate(
                    [jnp.broadcast_to(first[k : k + 1, cols], (8, 128)) for k in (i, i + 1)],
                    axis=0,
                )
            value = rt[rows, cols].astype(F32) + left * sjx[rows, cols]
            ct[rows, cols] = value.astype(BF)

    def main(lo, hi):
        for p in range(2):
            acc[p, :, lo:hi] = jnp.dot(
                ct[:, KH * p : KH * p + KH], bm[p, :, lo:hi], preferred_element_type=F32
            )

    core_copy = copy_to(partner, core_out, core_in, csend, crecv)

    def xy_copy(k):
        row, col = xy_peer(k)
        src = qb.at[
            pl.ds(pl.multiple_of(16 * row, 16), 16),
            pl.ds(pl.multiple_of(lax.rem(col // 2, 2) * 768, 128), 768),
        ]
        return copy_to((row, col), src, xy_in.at[k - 1], rsend.at[k - 1], rrecv.at[k - 1])

    wide = iota((PR, 128), 1)

    def start_of(a):
        return 0 if a == 0 else 768

    def summed_tile(a, n):
        n = n + start_of(a) // 128
        cols = slice(n * 128, n * 128 + 128)
        value = acc[0, :, cols]
        turned = pltpu.roll(acc[1, :, cols], 64, 1)
        after = 0.0
        if n < NW // 128 - 1:
            after = pltpu.roll(acc[1, :, n * 128 + 128 : n * 128 + 256], 64, 1)
        return value + jnp.where(wide < 64, turned, after)

    def give(a):
        for n in range(7):
            core_out[:, n * 128 : n * 128 + 128] = summed_tile(a, n).astype(BF)
        core_copy.start()

    def keep_own(a):
        for n in range(7):
            psum[:, n * 128 : n * 128 + 128] = summed_tile(a, n)

    def spread(a):
        core_copy.wait_recv()
        total = psum[...] + core_in[...].astype(F32)
        for yh in range(2):
            tiles = []
            for pair in range(4):
                sides = []
                for odd in range(2):
                    begin = NV * a - start_of(a) + 200 * pair + 100 * odd + 50 * yh
                    tile, s = begin // 128, begin % 128
                    by = (64 * odd - s) % 128
                    v = total[:, tile * 128 : tile * 128 + 128]
                    v = pltpu.roll(v, by, 1) if by else v
                    if s + 50 > 128:
                        u = total[:, tile * 128 + 128 : tile * 128 + 256]
                        u = pltpu.roll(u, by, 1) if by else u
                        v = jnp.where(wide < 64 * odd + 128 - s, v, u)
                    sides.append(v)
                v = jnp.where(wide < 64, sides[0], sides[1])
                tiles.append(v)
                cols = slice(yh * 768 + pair * 128, yh * 768 + pair * 128 + 128)
                qf[:, cols] = v[0:128, :]
                qb[:, cols] = v[0:128, :].astype(BF)
            for e in range(2):
                cols = slice(yh * 768 + 512 + e * 128, yh * 768 + 640 + e * 128)
                for i in range(PI):
                    v = jnp.concatenate(
                        [tiles[e + 2 * k][128 + 8 * i : 136 + 8 * i, :] for k in range(2)], axis=0
                    )
                    qf[16 * i : 16 * i + 16, cols] = v
                    qb[16 * i : 16 * i + 16, cols] = v.astype(BF)

        def start_xy(k, carry):
            xy_copy(k).start()
            return carry
        lax.fori_loop(1, 16, start_xy, 0)

    main(0, 1024)

    @pl.when(core == 1)
    def _():
        give(0)

    @pl.when(core == 0)
    def _():
        keep_own(0)

    main(1024, NW)

    @pl.when(core == 0)
    def _():
        give(1)
        spread(0)

    @pl.when(core == 1)
    def _():
        keep_own(1)
        spread(1)

    total = qf[
        pl.ds(pl.multiple_of(16 * r, 16), 16),
        pl.ds(pl.multiple_of(768 * y_hi, 128), 768),
    ]
    for k in range(1, 16):
        xy_copy(k).wait_recv()
        total = total + xy_in[k - 1].astype(F32)

    def z_copy(to, to_core):
        return copy_to(
            device(x, y, to, to_core), zb.at[to], z_in.at[core, z],
            zsend.at[to_core, to], zrecv.at[core, z],
        )

    zlane = iota((16, 128), 1)
    zsub = iota((16, 128), 0)
    for to in range(8):
        pair, odd = to // 2, to % 2
        early = total[:, pair * 128 : pair * 128 + 128]
        late8 = total[:, 512 + (pair % 2) * 128 : 640 + (pair % 2) * 128]
        if pair // 2:
            late8 = jnp.concatenate([late8[8:16, :], late8[0:8, :]], axis=0)
        if odd:
            early = pltpu.roll(early, 64, 1)
        else:
            late8 = pltpu.roll(late8, 64, 1)
        part = jnp.where(zlane < 64, early, jnp.where(zsub < 8, late8, 0.0))
        zf[to] = part
        zb[to] = part.astype(BF)
        for to_core in range(2):
            @pl.when(jnp.logical_not((z == to) & (core == to_core)))
            def _():
                z_copy(to, to_core).start()

    core_copy.wait_send()
    for k in range(1, 16):
        xy_copy(k).wait_send()
    z_in[core, z] = jnp.zeros((16, 128), BF)
    sums = []
    for a in range(2):
        value = jnp.where(core == a, zf[z], 0.0)
        for k in range(8):
            @pl.when(jnp.logical_not((z == k) & (core == a)))
            def _():
                copy_to(partner, zb.at[k], z_in.at[a, k], zsend.at[a, k], zrecv.at[a, k]).wait()
            value = value + z_in[a, k].astype(F32)
        sums.append(value.astype(BF))

    osub = iota((64, 128), 0)
    b_own = osub & 31
    wanted = ((osub >> 5) << 6) + core * VB + b_own
    select = one((iota((64, 128), 1) == wanted) & (b_own < VB))
    for a in range(2):
        narrow = lax.dot_general(
            select, sums[a], (((1,), (1,)), ((), ())), preferred_element_type=F32
        ).astype(BF)
        final = jnp.dot(narrow[0:32, :], expand[0:16, :], preferred_element_type=F32)
        final = final + jnp.dot(narrow[32:64, :], expand[16:32, :], preferred_element_type=F32)
        out[a] = final.astype(BF)[0:VB, 0:NOCC]


def run_round(index, amplitudes, singles_t, integrals, virt_irrep, occ_irrep):
    smem = pl.BlockSpec(memory_space=pltpu.SMEM)
    vmem = pl.BlockSpec(memory_space=pltpu.VMEM)
    hbm = pl.BlockSpec(memory_space=pl.ANY)
    dma = pltpu.SemaphoreType.DMA
    return pl.pallas_call(
        kernel,
        out_shape=(
            jax.ShapeDtypeStruct((2, VB, NOCC), BF),
            jax.ShapeDtypeStruct((1,), I32),
        ),
        in_specs=[smem, smem, smem, vmem, vmem, hbm, hbm],
        out_specs=(vmem, smem),
        scratch_shapes=[
            pltpu.VMEM((4, VB, ALEN), BF),
            pltpu.VMEM((BCH, VB, BLEN), BF),
            pltpu.VMEM((992, 128), I32),
            pltpu.VMEM((4, 992, 256), BF),
            pltpu.VMEM((KP, 256), BF),
            pltpu.VMEM((PR, KP), BF),
            pltpu.VMEM((PR, KP), BF),
            pltpu.VMEM((2, 4, 32, NW), BF),
            pltpu.VMEM((2, KH, NW), BF),
            pltpu.VMEM((PR, KP), F32),
            pltpu.VMEM((128, KP), BF),
            pltpu.VMEM((2, PR, NW), F32),
            pltpu.VMEM((PR, 896), F32),
            pltpu.VMEM((16, 128), BF),
            pltpu.VMEM((4, 16, 128), BF),
            pltpu.VMEM((32, 128), BF),
            pltpu.VMEM((PR, 896), BF),
            pltpu.VMEM((PR, 896), BF),
            pltpu.VMEM((128, 1536), F32),
            pltpu.VMEM((128, 1536), BF),
            pltpu.VMEM((15, 16, 768), BF),
            pltpu.VMEM((8, 16, 128), F32),
            pltpu.VMEM((8, 16, 128), BF),
            pltpu.VMEM((2, 8, 16, 128), BF),
            dma((4,)), dma((BCH,)), dma((16,)), dma((4,)), dma, dma,
            dma((15,)), dma((15,)), dma((2, 8)), dma((2, 8)),
        ],
        compiler_params=pltpu.CompilerParams(
            collective_id=0, has_side_effects=True, vmem_limit_bytes=58 * 1024 * 1024
        ),
        name="ladder_round",
    )(
        index, virt_irrep, occ_irrep, occ_irrep.reshape(1, NOCC), singles_t,
        amplitudes, integrals,
    )


def body(amplitudes, singles, integrals, virt_irrep, occ_irrep):
    singles_t = jnp.transpose(singles)

    def more(state):
        return state[0] < state[1][0]

    def step(state):
        index, _, total = state
        part, rounds = run_round(
            jnp.full((1,), index, I32), amplitudes, singles_t, integrals, virt_irrep, occ_irrep
        )
        return index + 1, rounds, total + part

    start = (jnp.int32(0), jnp.ones((1,), I32), jnp.zeros((2, VB, NOCC), BF))
    _, _, total = lax.while_loop(more, step, start)
    return jnp.transpose(total, (2, 0, 1))


def solution(mesh):
    placed = (P("col", "row"), P(None, "col"), P("col", "row"), P(), P())
    return jax.shard_map(
        body, mesh=mesh, in_specs=placed, out_specs=P("row", None, "col"), check_vma=False
    )
```

time: 510 us -> 42.6 us (0.08); the launches traced: 503 us -> 42.4 us
  waiting for transfers between devices: 281 us -> 0 us
  local copies, waits for them, and re-layouts: 78.7 us -> 0.62 us
  blocking collectives: 75.2 us -> 0 us
  other arithmetic: 41.3 us -> 0.73 us
  Pallas kernels: 0 us -> 40.4 us
  between operations: 14.9 us -> 0.01 us
  matrix products: 12.7 us -> 0 us
    unnamed x2 -> x0, waiting for transfers between devices: 281 us -> none
    all_gather x1 -> x0, blocking collectives: 46.9 us -> none  [body(): whole_singles = lax.all_gather(singles, 'col', axis=1, tiled=True)]
    pallas_call x0 -> x1, Pallas kernels: none -> 40.4 us  [run_round(): pl.pallas_call(kernel, out_shape=(jax.ShapeDtypeStruct((2, VB, NOCC), BF)...]
    unnamed x1 -> x0, blocking collectives: 28.3 us -> none
    gather x1 -> x0, other arithmetic: 21 us -> none  [body(): orbital_irrep = jnp.repeat(virt_irrep, VB, total_repeat_length=virt_total)]
    dot_general x2 -> x0, local copies, waits for them, and re-layouts: 19.1 us -> none  [body(): lax.dot_general(combined.reshape(second_width * first_width, pair_count),...]
    reshape x1 -> x0, local copies, waits for them, and re-layouts: 15.4 us -> none  [body(): integrals.reshape(second_width, first_width, panel_width * virt_total)]
    xor x10 -> x0, local copies, waits for them, and re-layouts: 14.7 us -> none  [the longest x4 14.2 us: body(): jnp.bitwise_xor(jnp.bitwise_xor(second_irrep[:, None, None], first_irrep[...]
  transfers between devices with their start and end apart: 1 -> 0, of which waited for: 1 -> 0; matrix products, arithmetic and copies ran while one was open for 0% -> 0% of each run, Pallas kernels for 0% -> 0%
where the time goes in v2:
time: 42.6 us; the launch traced here: 42.4 us
  Pallas kernels  40.4 us (95%)
  other arithmetic  0.73 us (2%)
  local copies, waits for them, and re-layouts  0.62 us (1%)
  loops' own time  0.62 us (1%)
    pallas_call x1, Pallas kernels, run_round(): pl.pallas_call(kernel, out_shape=(jax.ShapeDtypeStruct((2, VB, NOCC), BF)...  40.4 us

profile of v2, /device:TPU:1, one launch (start us, length us, event | category | flops | bytes accessed | tf_op | source)
XLA Modules:
  0.0 42.4 jit_solution(11951190036508785397)
XLA Ops:
  0.0 41.8 %while.12 = (s32[]{:T(128)}, s32[1]{0:T(128)}, bf16[2,25,100]{2,1,0:T(8,128)(2,1)S(1)}, s32[100]{0:T(128)}, s32[32]{0:T(128)}, /*index=5*/bf16[25,100]{1,0:T(8,1...) while((s32[]{:T(128)}, s32[1]{0:T(128)}, bf16[2,25,100]{2,1,0:T(8,128)(2,1)S(1)}, ...), condition=%wide.region_1.0_spmd, body=%wide.region_0.0_spmd.sunk | while | flops 5002 | bytes 30101 | solution.py:569
  0.0 40.4 %ladder_round.1 = (bf16[2,25,100]{2,1,0:T(8,128)(2,1)}, s32[1]{0:T(128)}) custom-call(s32[1]{0:T(128)} %bitcast.10.round_ref, s32[32]{0:T(128)} %get-tuple-element.140.virt, s32[100]{0:T(128)} %get-tuple-element.139.occ, s32[1,100]{1,0:T(1,128)} %bitcast.13, bf16[25,100]{1,0:T(8,128)(2,1)} %get-tuple-element.141.singles, ...), custom_call_target="tpu_custom_call" | custom-call | tf_op jit(solution)/shard_map/while/body/ladder_round/pallas_call | solution.py:509
  40.4 0.7 %add.9 = bf16[2,25,100]{2,1,0:T(8,128)(2,1)S(1)} add(bf16[2,25,100]{2,1,0:T(8,128)(2,1)S(1)} %get-tuple-element.129, bf16[2,25,100]{2,1,0:T(8,128)(2,1)} %get-tuple-element.117) | non-fusion elementwise | flops 5000 | bytes 30000 | tf_op jit(solution)/shard_map/while/body/add | solution.py:566
  41.8 0.6 %copy.8 = bf16[2,25,100]{2,0,1:T(2,128)(2,1)} copy(bf16[2,25,100]{2,1,0:T(8,128)(2,1)S(1)} %get-tuple-element.49) | data formatting | bytes 20000 | tf_op jit(solution)/shard_map/while | solution.py:569
  (1 shorter events, 0.0 us)

commit v3 on v2

--- a/solution.py
+++ b/solution.py
@@ -28,6 +28,8 @@
 BLEN = 20 * 1600
 NW = 13 * 128
 NV = 800
+Z_ORDER = (4, 3, 5, 2, 6, 1, 7)
+XY_ORDER = (10, 6, 9, 11, 14, 2, 5, 7, 8, 13, 15, 1, 3, 4, 12)
 
 
 def iota(shape, dim):
@@ -90,38 +92,28 @@
     def greet(where):
         pl.semaphore_signal(barrier, inc=1, device_id=where, device_id_type=MESH)
 
-    for sy in (y, 3 - y):
+    def wrap(v, n):
+        return jnp.where(v >= n, v - n, v)
+
+    def z_peer(k, to_core):
+        return device(x, y, wrap(z + k, 8), to_core)
+
+    def xy_peer(k):
+        return device(wrap(x + k % 4, 4), wrap(y + k // 4, 4), z, core)
+
+    partner = device(x, y, z, 1 - core)
+
+    for sc in range(2):
+        greet(device(x, 3 - y, r, sc))
+    for sc in range(2):
+        @pl.when(jnp.logical_not(at_home & (sc == core)))
+        def _():
+            greet(device(x, y, r, sc))
+    for k in Z_ORDER:
         for sc in range(2):
-            me = at_home & (sc == core) if sy is y else False
-            if sy is y:
-                @pl.when(jnp.logical_not(me))
-                def _():
-                    greet(device(x, sy, r, sc))
-            else:
-                greet(device(x, sy, r, sc))
-
-    def z_peer(k):
-        return device(x, y, lax.rem(z + k, 8), core)
-
-    def z_cross(k):
-        return device(x, y, lax.rem(z + k, 8), 1 - core)
-
-    def xy_peer(k):
-        return device(lax.rem(x + lax.rem(k, 4), 4), lax.rem(y + k // 4, 4), z, core)
-
-    partner = device(x, y, z, 1 - core)
-
-    def greet_z(k, carry):
-        greet(z_peer(k))
-        greet(z_cross(k))
-        return carry
-
-    def greet_xy(k, carry):
+            greet(z_peer(k, sc))
+    for k in XY_ORDER:
         greet(xy_peer(k))
-        return carry
-
-    lax.fori_loop(1, 8, greet_z, 0)
-    lax.fori_loop(1, 16, greet_xy, 0)
     greet(partner)
 
     first_rank = round_ref[0] * SLOT
@@ -199,35 +191,36 @@
 
     lax.fori_loop(0, 4, compact, 0)
 
+    pl.semaphore_wait(
+        barrier,
+        30 + jnp.where(is_source, 16, 0) - jnp.where(is_source & at_home, 1, 0),
+    )
+
+    def singles_copy(k, tc):
+        return copy_to(
+            device(x, target_y, wrap(z + k, 8), tc), s_own, s_in.at[my_q],
+            ssend.at[2 * k + tc], srecv.at[my_q],
+        )
+
+    def for_targets(act):
+        for k in Z_ORDER:
+            for tc in range(2):
+                act(singles_copy(k, tc))
+        for tc in range(2):
+            @pl.when(jnp.logical_not(at_home & (tc == core)))
+            def _():
+                act(singles_copy(0, tc))
+
+    @pl.when(is_source)
+    def _():
+        for_targets(lambda copy: copy.start())
+
     def turn(step, carry):
         at = pl.multiple_of(step * 256, 256)
         rt[:, pl.ds(at, 256)] = cs[pl.ds(at, 256), :].T[0:PR, :]
         return carry
 
     lax.fori_loop(0, KP // 256, turn, 0)
-
-    pl.semaphore_wait(
-        barrier,
-        30 + jnp.where(is_source, 16, 0) - jnp.where(is_source & at_home, 1, 0),
-    )
-
-    def singles_copy(k):
-        tz, tc = k // 2, lax.rem(k, 2)
-        return copy_to(
-            device(x, target_y, tz, tc), s_own, s_in.at[my_q], ssend.at[k], srecv.at[my_q]
-        )
-
-    def not_me(k):
-        return jnp.logical_not(at_home & (k // 2 == z) & (lax.rem(k, 2) == core))
-
-    @pl.when(is_source)
-    def _():
-        def send(k, carry):
-            @pl.when(not_me(k))
-            def _():
-                singles_copy(k).start()
-            return carry
-        lax.fori_loop(0, 16, send, 0)
 
     for p in range(2):
         col_at = iota((8, NW), 1) - 64 * p
@@ -240,26 +233,6 @@
         for q in range(4):
             want = g_zero ^ g_own ^ virt[4 * r + q]
             masks[p, q] = one(jnp.broadcast_to(g_lane[0:1, :], (32, NW)) == want)
-
-    for p in range(2):
-        bm[p, 1600:KH, :] = jnp.zeros((KH - 1600, NW), BF)
-
-    def arrange(k, carry):
-        @pl.when(lax.rem(k, 10) == 0)
-        def _():
-            int_copy(k // 10).wait()
-        ch, w = k // 10, lax.rem(k, 10)
-        row = pl.multiple_of(32 * k, 32)
-        for p in range(2):
-            q = (2 * k + p) // 25
-            for n in range(13):
-                v = bv[ch, :, pl.ds(pl.multiple_of(128 * (25 * w + 12 * p + n), 128), 128)]
-                ok = masks[p, q, 0:VB, n * 128 : n * 128 + 128] > 0
-                v = jnp.where(ok, v, jnp.zeros_like(v))
-                bm[p, pl.ds(row, 32), n * 128 : n * 128 + 128] = pad_rows(v)
-        return carry
-
-    lax.fori_loop(0, NC // 2, arrange, 0)
 
     prow = iota((PR, 128), 0)
     late = prow >= 128
@@ -302,14 +275,37 @@
     )
     expand[...] = one(keep)
 
+    for p in range(2):
+        bm[p, 1600:KH, :] = jnp.zeros((KH - 1600, NW), BF)
+
+    def arrange(lo, hi):
+        def step(n, carry):
+            at = pl.multiple_of(n * 128, 128)
+            for p in range(2):
+                for q in range(4):
+                    ks = [k for k in range(lo, hi) if (2 * k + p) // VB == q]
+                    if not ks:
+                        continue
+                    ok = masks[p, q, 0:VB, pl.ds(at, 128)] > 0
+                    for k in ks:
+                        from_at = pl.multiple_of(128 * (25 * (k % 10) + 12 * p) + at, 128)
+                        v = bv[k // 10, :, pl.ds(from_at, 128)]
+                        v = jnp.where(ok, v, jnp.zeros_like(v))
+                        bm[p, 32 * k : 32 * k + 32, pl.ds(at, 128)] = pad_rows(v)
+            return carry
+        lax.fori_loop(0, NW // 128, step, 0)
+
+    for k in range(2):
+        int_copy(k).wait()
+    arrange(0, 20)
+
+    for k in range(2, BCH):
+        int_copy(k).wait()
+    arrange(20, 50)
+
     @pl.when(is_source)
     def _():
-        def sent(k, carry):
-            @pl.when(not_me(k))
-            def _():
-                singles_copy(k).wait_send()
-            return carry
-        lax.fori_loop(0, 16, sent, 0)
+        for_targets(lambda copy: copy.wait_send())
 
     for t in range(4):
         me = at_home & (my_q == t)
@@ -413,10 +409,8 @@
                     qf[16 * i : 16 * i + 16, cols] = v
                     qb[16 * i : 16 * i + 16, cols] = v.astype(BF)
 
-        def start_xy(k, carry):
+        for k in XY_ORDER:
             xy_copy(k).start()
-            return carry
-        lax.fori_loop(1, 16, start_xy, 0)
 
     main(0, 1024)
 
@@ -444,14 +438,15 @@
         pl.ds(pl.multiple_of(16 * r, 16), 16),
         pl.ds(pl.multiple_of(768 * y_hi, 128), 768),
     ]
-    for k in range(1, 16):
+    for k in XY_ORDER[::-1]:
         xy_copy(k).wait_recv()
         total = total + xy_in[k - 1].astype(F32)
 
-    def z_copy(to, to_core):
+    def z_copy(k, to_core):
+        to = wrap(z + k, 8)
         return copy_to(
             device(x, y, to, to_core), zb.at[to], z_in.at[core, z],
-            zsend.at[to_core, to], zrecv.at[core, z],
+            zsend.at[to_core, k], zrecv.at[core, z],
         )
 
     zlane = iota((16, 128), 1)
@@ -469,24 +464,32 @@
         part = jnp.where(zlane < 64, early, jnp.where(zsub < 8, late8, 0.0))
         zf[to] = part
         zb[to] = part.astype(BF)
+    for k in Z_ORDER:
         for to_core in range(2):
-            @pl.when(jnp.logical_not((z == to) & (core == to_core)))
-            def _():
-                z_copy(to, to_core).start()
+            z_copy(k, to_core).start()
+    partner_copy = copy_to(
+        partner, zb.at[z], z_in.at[core, z], zsend.at[0, 0], zrecv.at[core, z]
+    )
+    partner_copy.start()
 
     core_copy.wait_send()
     for k in range(1, 16):
         xy_copy(k).wait_send()
-    z_in[core, z] = jnp.zeros((16, 128), BF)
-    sums = []
-    for a in range(2):
-        value = jnp.where(core == a, zf[z], 0.0)
-        for k in range(8):
-            @pl.when(jnp.logical_not((z == k) & (core == a)))
-            def _():
-                copy_to(partner, zb.at[k], z_in.at[a, k], zsend.at[a, k], zrecv.at[a, k]).wait()
-            value = value + z_in[a, k].astype(F32)
-        sums.append(value.astype(BF))
+    partner_copy.wait_send()
+    copy_to(
+        partner, zb.at[z], z_in.at[1 - core, z], zsend.at[0, 0], zrecv.at[1 - core, z]
+    ).wait_recv()
+    own, other = zf[z], z_in[1 - core, z].astype(F32)
+    sums = [jnp.where(core == a, own, other) for a in range(2)]
+    for k in Z_ORDER[::-1]:
+        origin = wrap(z + (8 - k), 8)
+        for a in range(2):
+            z_copy(k, a).wait_send()
+            copy_to(
+                partner, zb.at[z], z_in.at[a, origin], zsend.at[a, k], zrecv.at[a, origin]
+            ).wait_recv()
+            sums[a] = sums[a] + z_in[a, origin].astype(F32)
+    sums = [v.astype(BF) for v in sums]
 
     osub = iota((64, 128), 0)
     b_own = osub & 31

time: 42.6 us -> 39.1 us (0.918)
  Pallas kernels: 40.4 us -> 36.9 us
    pallas_call x1, Pallas kernels: 40.4 us -> 36.9 us  [run_round(): pl.pallas_call(kernel, out_shape=(jax.ShapeDtypeStruct((2, VB, NOCC), BF)...]
where the time goes in v3:
time: 39.1 us; the launch traced here: 38.9 us
  Pallas kernels  36.9 us (94%)
  other arithmetic  0.73 us (2%)
  local copies, waits for them, and re-layouts  0.62 us (2%)
  loops' own time  0.62 us (2%)
    pallas_call x1, Pallas kernels, run_round(): pl.pallas_call(kernel, out_shape=(jax.ShapeDtypeStruct((2, VB, NOCC), BF)...  36.9 us

profile of v3, /device:TPU:1, one launch (start us, length us, event | category | flops | bytes accessed | tf_op | source)
XLA Modules:
  0.0 38.9 jit_solution(4306873204881836264)
XLA Ops:
  0.0 38.2 %while.12 = (s32[]{:T(128)}, s32[1]{0:T(128)}, bf16[2,25,100]{2,1,0:T(8,128)(2,1)S(1)}, s32[100]{0:T(128)}, s32[32]{0:T(128)}, /*index=5*/bf16[25,100]{1,0:T(8,1...) while((s32[]{:T(128)}, s32[1]{0:T(128)}, bf16[2,25,100]{2,1,0:T(8,128)(2,1)S(1)}, ...), condition=%wide.region_1.0_spmd, body=%wide.region_0.0_spmd.sunk | while | flops 5002 | bytes 30101 | solution.py:572
  0.0 36.9 %ladder_round.1 = (bf16[2,25,100]{2,1,0:T(8,128)(2,1)}, s32[1]{0:T(128)}) custom-call(s32[1]{0:T(128)} %bitcast.10.round_ref, s32[32]{0:T(128)} %get-tuple-element.140.virt, s32[100]{0:T(128)} %get-tuple-element.139.occ, s32[1,100]{1,0:T(1,128)} %bitcast.13, bf16[25,100]{1,0:T(8,128)(2,1)} %get-tuple-element.141.singles, ...), custom_call_target="tpu_custom_call" | custom-call | tf_op jit(solution)/shard_map/while/body/ladder_round/pallas_call | solution.py:512
  36.9 0.7 %add.9 = bf16[2,25,100]{2,1,0:T(8,128)(2,1)S(1)} add(bf16[2,25,100]{2,1,0:T(8,128)(2,1)S(1)} %get-tuple-element.129, bf16[2,25,100]{2,1,0:T(8,128)(2,1)} %get-tuple-element.117) | non-fusion elementwise | flops 5000 | bytes 30000 | tf_op jit(solution)/shard_map/while/body/add | solution.py:569
  38.3 0.6 %copy.8 = bf16[2,25,100]{2,0,1:T(2,128)(2,1)} copy(bf16[2,25,100]{2,1,0:T(8,128)(2,1)S(1)} %get-tuple-element.49) | data formatting | bytes 20000 | tf_op jit(solution)/shard_map/while | solution.py:572
  (1 shorter events, 0.0 us)

commit v4 on v3

--- a/solution.py
+++ b/solution.py
@@ -69,21 +69,6 @@
             device_id=where, device_id_type=MESH,
         )
 
-    def amp_copy(q):
-        return pltpu.make_async_copy(
-            amp.at[:, pl.ds(pl.multiple_of(q * (156 * 128), 128), ALEN)], av.at[q], asem.at[q]
-        )
-
-    def int_copy(k):
-        return pltpu.make_async_copy(
-            integ.at[:, pl.ds(pl.multiple_of(k * BLEN, 128), BLEN)], bv.at[k], bsem.at[k]
-        )
-
-    for q in range(4):
-        amp_copy(q).start()
-    for k in range(BCH):
-        int_copy(k).start()
-
     barrier = pltpu.get_barrier_semaphore()
     at_home = r == z
     is_source = x == lax.rem(z, 4)
@@ -109,6 +94,21 @@
         @pl.when(jnp.logical_not(at_home & (sc == core)))
         def _():
             greet(device(x, y, r, sc))
+    def amp_copy(q):
+        return pltpu.make_async_copy(
+            amp.at[:, pl.ds(pl.multiple_of(q * (156 * 128), 128), ALEN)], av.at[q], asem.at[q]
+        )
+
+    def int_copy(k):
+        return pltpu.make_async_copy(
+            integ.at[:, pl.ds(pl.multiple_of(k * BLEN, 128), BLEN)], bv.at[k], bsem.at[k]
+        )
+
+    for q in range(4):
+        amp_copy(q).start()
+    for k in range(BCH):
+        int_copy(k).start()
+
     for k in Z_ORDER:
         for sc in range(2):
             greet(z_peer(k, sc))

time: 39.1 us -> 39.2 us (level)
  no operation moved by 1% of the time
where the time goes in v4:
time: 39.2 us; the launch traced here: 38.9 us
  Pallas kernels  37 us (94%)
  other arithmetic  0.73 us (2%)
  local copies, waits for them, and re-layouts  0.62 us (2%)
  loops' own time  0.62 us (2%)
    pallas_call x1, Pallas kernels, run_round(): pl.pallas_call(kernel, out_shape=(jax.ShapeDtypeStruct((2, VB, NOCC), BF)...  37 us

profile of v4, /device:TPU:1, one launch (start us, length us, event | category | flops | bytes accessed | tf_op | source)
XLA Modules:
  0.0 38.9 jit_solution(16297808971503691182)
XLA Ops:
  0.0 38.3 %while.12 = (s32[]{:T(128)}, s32[1]{0:T(128)}, bf16[2,25,100]{2,1,0:T(8,128)(2,1)S(1)}, s32[100]{0:T(128)}, s32[32]{0:T(128)}, /*index=5*/bf16[25,100]{1,0:T(8,1...) while((s32[]{:T(128)}, s32[1]{0:T(128)}, bf16[2,25,100]{2,1,0:T(8,128)(2,1)S(1)}, ...), condition=%wide.region_1.0_spmd, body=%wide.region_0.0_spmd.sunk | while | flops 5002 | bytes 30101 | solution.py:572
  0.0 37.0 %ladder_round.1 = (bf16[2,25,100]{2,1,0:T(8,128)(2,1)}, s32[1]{0:T(128)}) custom-call(s32[1]{0:T(128)} %bitcast.10.round_ref, s32[32]{0:T(128)} %get-tuple-element.140.virt, s32[100]{0:T(128)} %get-tuple-element.139.occ, s32[1,100]{1,0:T(1,128)} %bitcast.13, bf16[25,100]{1,0:T(8,128)(2,1)} %get-tuple-element.141.singles, ...), custom_call_target="tpu_custom_call" | custom-call | tf_op jit(solution)/shard_map/while/body/ladder_round/pallas_call | solution.py:512
  37.0 0.7 %add.9 = bf16[2,25,100]{2,1,0:T(8,128)(2,1)S(1)} add(bf16[2,25,100]{2,1,0:T(8,128)(2,1)S(1)} %get-tuple-element.129, bf16[2,25,100]{2,1,0:T(8,128)(2,1)} %get-tuple-element.117) | non-fusion elementwise | flops 5000 | bytes 30000 | tf_op jit(solution)/shard_map/while/body/add | solution.py:569
  38.3 0.6 %copy.8 = bf16[2,25,100]{2,0,1:T(2,128)(2,1)} copy(bf16[2,25,100]{2,1,0:T(8,128)(2,1)S(1)} %get-tuple-element.49) | data formatting | bytes 20000 | tf_op jit(solution)/shard_map/while | solution.py:572
  (1 shorter events, 0.0 us)
